TPU v7x, 32 devices: a whole 2x2x4 slice. The times are simulated.
32 devices in a mesh: rad: 4 (over y, core), azi: 8 (over z, x).
Axes of the slice: x: 2, y: 2, z: 4, core: 2. Of those that a mesh axis runs over, the one named last changes fastest.
Arguments:
- fields: float32 [5, 8, 512, 512], P(None, None, 'azi', 'rad'), may hold values from -6 to 6
- radial_metric: float32 [512], P('rad'), may hold values from 0.5 to 2
- azimuth_metric: float32 [512], P('rad'), may hold values from 0.5 to 2
Outputs:
- grad_azimuth: float32 [5, 8, 512, 512], P(None, None, 'azi', 'rad')
- grad_radial: float32 [5, 8, 512, 512], P(None, None, 'azi', 'rad')
- filtered: float32 [5, 8, 512, 512], P(None, None, 'azi', 'rad')
All inputs are finite; a program needn't handle non-finite values.
Results may differ from a plain program's by a relative error of at most 0.0003.
Values sent between devices are 32-bit elements; how exact they have to be, the bound alone decides.
A program may use at most 192 MiB of HBM per device.

v0:
```python
import jax
import jax.numpy as jnp
from jax import lax
from jax.sharding import PartitionSpec as P

ALPHA_D = 1.0 / 3.0
COEF_A = 14.0 / 9.0
COEF_B = 1.0 / 9.0
ALPHA_F = 0.49
HIGHEST = lax.Precision.HIGHEST


def extended(block, sides, width, periodic):
    for axis, dim in sides:
        count = lax.axis_size(axis)
        forward = [(i, i + 1) for i in range(count - 1)]
        if periodic:
            forward.append((count - 1, 0))
        backward = [(target, source) for source, target in forward]
        low = lax.ppermute(
            lax.slice_in_dim(block, block.shape[dim] - width, None, axis=dim), axis, forward
        )
        high = lax.ppermute(lax.slice_in_dim(block, 0, width, axis=dim), axis, backward)
        block = jnp.concatenate([low, block, high], axis=dim)
    return block


def filter_weights():
    slack = 1.0 - 2.0 * ALPHA_F
    return [
        (193.0 + 126.0 * ALPHA_F) / 256.0,
        (105.0 + 302.0 * ALPHA_F) / 256.0,
        -15.0 * slack / 64.0,
        45.0 * slack / 512.0,
        -5.0 * slack / 256.0,
        slack / 512.0,
    ]


def local_tables(cells, alpha):
    lower = jnp.full((cells,), alpha, jnp.float32).at[0].set(0.0)
    upper = jnp.full((cells,), alpha, jnp.float32).at[cells - 1].set(0.0)
    middle = jnp.ones((cells,), jnp.float32)
    inverse = lax.linalg.tridiagonal_solve(lower, middle, upper, jnp.eye(cells, dtype=jnp.float32))
    head_col = inverse[:, 0]
    tail_col = inverse[:, cells - 1]
    tail_gain = alpha * inverse[cells - 1, cells - 1]
    head_gain = alpha * inverse[0, 0]
    return (inverse, head_col, tail_col, tail_gain, head_gain)


def neighbour_bounds(padded, tail_gain, head_gain):
    det = 1.0 - tail_gain * head_gain
    left_value = (padded[0] - tail_gain * padded[1]) / det
    right_value = (padded[3] - head_gain * padded[2]) / det
    return (left_value, right_value)


def local(fields, radial_metric, azimuth_metric):
    rad_count = lax.axis_size("rad")
    cells_t = fields.shape[2]
    cells_r = fields.shape[3]
    padded = extended(fields, (("azi", 2),), 5, True)

    def along(offset):
        return lax.slice_in_dim(padded, 5 + offset, 5 + offset + cells_t, axis=2)

    slope_side = 0.5 * COEF_A * (along(1) - along(-1)) + 0.25 * COEF_B * (along(2) - along(-2))
    weights = filter_weights()
    smooth_side = weights[0] * fields
    for offset in range(1, 6):
        smooth_side = smooth_side + 0.5 * weights[offset] * (along(offset) + along(-offset))
    slope_inv, slope_head, slope_tail, slope_tg, slope_hg = local_tables(cells_t, ALPHA_D)
    smooth_inv, smooth_head, smooth_tail, smooth_tg, smooth_hg = local_tables(cells_t, ALPHA_F)
    slope_loc = jnp.einsum("ij,fajr->fair", slope_inv, slope_side, precision=HIGHEST)
    smooth_loc = jnp.einsum("ij,fajr->fair", smooth_inv, smooth_side, precision=HIGHEST)
    slope_edges = jnp.stack([slope_loc[:, :, 0, :], slope_loc[:, :, cells_t - 1, :]], axis=2)
    smooth_edges = jnp.stack([smooth_loc[:, :, 0, :], smooth_loc[:, :, cells_t - 1, :]], axis=2)
    edges = jnp.concatenate([slope_edges, smooth_edges], axis=3)
    rimmed = extended(edges, (("azi", 2),), 1, True)
    rimmed = jnp.moveaxis(rimmed, 2, 0)
    slope_left, slope_right = neighbour_bounds(rimmed[:, :, :, :cells_r], slope_tg, slope_hg)
    smooth_left, smooth_right = neighbour_bounds(rimmed[:, :, :, cells_r:], smooth_tg, smooth_hg)
    slope_azi = slope_loc - ALPHA_D * (
        slope_left[:, :, None, :] * slope_head[None, None, :, None]
        + slope_right[:, :, None, :] * slope_tail[None, None, :, None]
    )
    smoothed = smooth_loc - ALPHA_F * (
        smooth_left[:, :, None, :] * smooth_head[None, None, :, None]
        + smooth_right[:, :, None, :] * smooth_tail[None, None, :, None]
    )
    radial_padded = extended(fields, (("rad", 3),), 2, False)

    def radial(offset):
        return lax.slice_in_dim(radial_padded, 2 + offset, 2 + offset + cells_r, axis=3)

    radial_side = 0.5 * COEF_A * (radial(1) - radial(-1)) + 0.25 * COEF_B * (radial(2) - radial(-2))
    radial_inv, radial_head, radial_tail, radial_tg, radial_hg = local_tables(cells_r, ALPHA_D)
    radial_loc = jnp.einsum("ij,fatj->fati", radial_inv, radial_side, precision=HIGHEST)
    radial_edges = jnp.stack([radial_loc[:, :, :, 0], radial_loc[:, :, :, cells_r - 1]], axis=2)
    radial_rimmed = extended(radial_edges, (("rad", 2),), 1, False)
    radial_rimmed = jnp.moveaxis(radial_rimmed, 2, 0)
    place = lax.axis_index("rad")
    has_before = (place > 0).astype(jnp.float32)
    has_after = (place < rad_count - 1).astype(jnp.float32)
    radial_left, radial_right = neighbour_bounds(radial_rimmed, radial_tg, radial_hg)
    radial_left = has_before * radial_left
    radial_right = has_after * radial_right
    slope_rad = radial_loc - ALPHA_D * (
        radial_left[:, :, :, None] * radial_head + radial_right[:, :, :, None] * radial_tail
    )
    return (slope_azi * azimuth_metric, slope_rad * radial_metric, smoothed)


def solution(mesh):
    in_specs = (P(None, None, "azi", "rad"), P("rad"), P("rad"))
    out_specs = (
        P(None, None, "azi", "rad"),
        P(None, None, "azi", "rad"),
        P(None, None, "azi", "rad"),
    )
    return jax.shard_map(local, mesh=mesh, in_specs=in_specs, out_specs=out_specs, check_vma=False)
```

profile of v0, /device:TPU:1, one launch (start us, length us, event | category | flops | bytes accessed | tf_op | source)
XLA Modules:
  0.0 174.3 jit_solution(11154079368688959212)
XLA Ops:
  3.8 3.1 %collective-permute-start = (f32[5,8,5,128]{3,2,1,0:T(8,128)S(1)}, f32[5,8,5,128]{3,2,1,0:T(8,128)S(1)}, u32[]{:S(2)}, u32[]{:S(2)}) collective-permute-start(f32[5,8,5,128]{3,2,1,0:T(8,128)S(1)} %get-tuple-element.742), channel_id=1, source_target_pairs={{1,0},{2,1},{3,2},{4,3},{5,4},{6,5},{7,6},{0,7},{9,8},{10,9},{11,1... | collective-permute-start | bytes 307208 | tf_op jit(solution)/shard_map/ppermute | solution.py:23
  9.6 4.1 %collective-permute-start.5 = (f32[5,8,64,2]{2,1,3,0:T(8,128)S(1)}, f32[5,8,64,2]{2,1,3,0:T(8,128)S(1)}, u32[]{:S(2)}, u32[]{:S(2)}) collective-permute-start(f32[5,8,64,2]{2,1,3,0:T(8,128)S(1)} %copy.15), channel_id=1, source_target_pairs={{0,8},{8,16},{16,24},{1,9},{9,17},{17,25},{2,10},{10,18},{18,26},{... | collective-permute-start | bytes 61448 | tf_op jit(solution)/shard_map/ppermute | solution.py:20
  16.9 5.7 %while.28 = (s32[]{:T(128)}, f32[]{:T(128)}, f32[128]{0:T(128)S(1)}, f32[3,32]{1,0:T(4,128)S(1)}, f32[3,32,128]{2,1,0:T(8,128)S(1)}, /*index=5*/f32[3,32,128]{2,...) while((s32[]{:T(128)}, f32[]{:T(128)}, ...), condition=%wide.region_1.0_spmd, body=%wide.region_0.0_spmd.sunk | while | flops 12417 | bytes 102505 | solution.py:44
  27.3 64.4 %while.29 = (s32[]{:T(128)}, f32[128]{0:T(128)S(1)}, f32[3,32,128]{2,1,0:T(8,128)S(1)}, f32[3,32,128]{2,1,0:T(8,128)S(1)}, f32[3,32]{1,0:T(4,128)S(1)}, /*index=...) while((s32[]{:T(128)}, f32[128]{0:T(128)S(1)}, ...), condition=%wide.region_3.4_spmd, body=%wide.region_2.3_spmd.sunk | while | flops 8226 | bytes 101333 | solution.py:44
  28.8 19.9 %fusion.695 = (f32[128]{0:T(128)S(1)}, f32[128]{0:T(128)S(1)}, f32[128]{0:T(128)S(1)}, f32[128]{0:T(128)S(1)}, f32[128]{0:T(128)S(1)}, /*index=5*/f32[128]{0:T(1...) fusion(f32[3,32,128]{2,1,0:T(8,128)S(1)} %get-tuple-element.125, ...), kind=kLoop, calls=%fused_computation.166.clone.1 | loop fusion | flops 8192 | bytes 33536 | tf_op jit(solution)/shard_map/while/body/eval_jaxpr/sub | solution.py:44
  50.3 19.9 %fusion.695 = (f32[128]{0:T(128)S(1)}, f32[128]{0:T(128)S(1)}, f32[128]{0:T(128)S(1)}, f32[128]{0:T(128)S(1)}, f32[128]{0:T(128)S(1)}, /*index=5*/f32[128]{0:T(1...) fusion(f32[3,32,128]{2,1,0:T(8,128)S(1)} %get-tuple-element.125, ...), kind=kLoop, calls=%fused_computation.166.clone.1 | loop fusion | flops 8192 | bytes 33536 | tf_op jit(solution)/shard_map/while/body/eval_jaxpr/sub | solution.py:44
  71.7 19.9 %fusion.695 = (f32[128]{0:T(128)S(1)}, f32[128]{0:T(128)S(1)}, f32[128]{0:T(128)S(1)}, f32[128]{0:T(128)S(1)}, f32[128]{0:T(128)S(1)}, /*index=5*/f32[128]{0:T(1...) fusion(f32[3,32,128]{2,1,0:T(8,128)S(1)} %get-tuple-element.125, ...), kind=kLoop, calls=%fused_computation.166.clone.1 | loop fusion | flops 8192 | bytes 33536 | tf_op jit(solution)/shard_map/while/body/eval_jaxpr/sub | solution.py:44
  93.0 2.7 %fusion.528 = (f32[1,128]{1,0:T(1,128)S(1)}, f32[128]{0:T(128)S(1)}) fusion(f32[]{:T(128)} %bitcast.377, f32[96,128]{1,0:T(8,128)} %bitcast.2570, f32[128]{0:T(128)S(1)} %get-tuple-element.437, f32[]{:T(128)} %bitcast.381, f32[]{:T(128)} %bitcast.379), kind=kLoop, calls=%fused_computation.1023 | loop fusion | flops 768 | bytes 3084 | tf_op jit(solution)/shard_map/broadcast_in_dim | solution.py:44
  95.7 2.8 %fusion.527 = (f32[1,128]{1,0:T(1,128)S(1)}, f32[128]{0:T(128)S(1)}) fusion(f32[]{:T(128)} %bitcast.373, f32[96,128]{1,0:T(8,128)} %bitcast.2571, f32[128]{0:T(128)S(1)} %get-tuple-element.439, f32[]{:T(128)} %bitcast.377, f32[]{:T(128)} %bitcast.375), kind=kLoop, calls=%fused_computation.1022 | loop fusion | flops 768 | bytes 3084 | tf_op jit(solution)/shard_map/broadcast_in_dim | solution.py:44
  98.5 2.8 %fusion.526 = (f32[1,128]{1,0:T(1,128)S(1)}, f32[128]{0:T(128)S(1)}) fusion(f32[]{:T(128)} %bitcast.369, f32[96,128]{1,0:T(8,128)} %bitcast.2572, f32[128]{0:T(128)S(1)} %get-tuple-element.441, f32[]{:T(128)} %bitcast.373, f32[]{:T(128)} %bitcast.371), kind=kLoop, calls=%fused_computation.1021 | loop fusion | flops 768 | bytes 3084 | tf_op jit(solution)/shard_map/broadcast_in_dim | solution.py:44
  101.3 2.7 %fusion.525 = (f32[1,128]{1,0:T(1,128)S(1)}, f32[128]{0:T(128)S(1)}) fusion(f32[]{:T(128)} %bitcast.365, f32[96,128]{1,0:T(8,128)} %bitcast.2573, f32[128]{0:T(128)S(1)} %get-tuple-element.443, f32[]{:T(128)} %bitcast.369, f32[]{:T(128)} %bitcast.367), kind=kLoop, calls=%fused_computation.1020 | loop fusion | flops 768 | bytes 3084 | tf_op jit(solution)/shard_map/broadcast_in_dim | solution.py:44
  104.0 2.7 %fusion.524 = (f32[1,128]{1,0:T(1,128)S(1)}, f32[128]{0:T(128)S(1)}) fusion(f32[]{:T(128)} %bitcast.361, f32[96,128]{1,0:T(8,128)} %bitcast.2574, f32[128]{0:T(128)S(1)} %get-tuple-element.445, f32[]{:T(128)} %bitcast.365, f32[]{:T(128)} %bitcast.363), kind=kLoop, calls=%fused_computation.1019 | loop fusion | flops 768 | bytes 3084 | tf_op jit(solution)/shard_map/broadcast_in_dim | solution.py:44
  109.3 2.6 %fusion.522 = (f32[1,128]{1,0:T(1,128)S(1)}, f32[128]{0:T(128)S(1)}) fusion(f32[]{:T(128)} %bitcast.353, f32[96,128]{1,0:T(8,128)} %bitcast.2576, f32[128]{0:T(128)S(1)} %get-tuple-element.449, f32[]{:T(128)} %bitcast.357, f32[]{:T(128)} %bitcast.355), kind=kLoop, calls=%fused_computation.1017 | loop fusion | flops 768 | bytes 3084 | tf_op jit(solution)/shard_map/broadcast_in_dim | solution.py:44
  111.9 2.6 %fusion.521 = (f32[1,128]{1,0:T(1,128)S(1)}, f32[128]{0:T(128)S(1)}) fusion(f32[]{:T(128)} %bitcast.349, f32[96,128]{1,0:T(8,128)} %bitcast.2577, f32[128]{0:T(128)S(1)} %get-tuple-element.451, f32[]{:T(128)} %bitcast.353, f32[]{:T(128)} %bitcast.351), kind=kLoop, calls=%fused_computation.1016 | loop fusion | flops 768 | bytes 3084 | tf_op jit(solution)/shard_map/broadcast_in_dim | solution.py:44
  114.5 2.6 %fusion.520 = (f32[1,128]{1,0:T(1,128)S(1)}, f32[128]{0:T(128)S(1)}) fusion(f32[]{:T(128)} %bitcast.345, f32[96,128]{1,0:T(8,128)} %bitcast.2578, f32[128]{0:T(128)S(1)} %get-tuple-element.453, f32[]{:T(128)} %bitcast.349, f32[]{:T(128)} %bitcast.347), kind=kLoop, calls=%fused_computation.1015 | loop fusion | flops 768 | bytes 3084 | tf_op jit(solution)/shard_map/broadcast_in_dim | solution.py:44
  117.1 2.6 %fusion.519 = (f32[1,128]{1,0:T(1,128)S(1)}, f32[128]{0:T(128)S(1)}) fusion(f32[]{:T(128)} %bitcast.341, f32[96,128]{1,0:T(8,128)} %bitcast.2579, f32[128]{0:T(128)S(1)} %get-tuple-element.455, f32[]{:T(128)} %bitcast.345, f32[]{:T(128)} %bitcast.343), kind=kLoop, calls=%fused_computation.1014 | loop fusion | flops 768 | bytes 3084 | tf_op jit(solution)/shard_map/broadcast_in_dim | solution.py:44
  119.7 2.7 %fusion.518 = (f32[1,128]{1,0:T(1,128)S(1)}, f32[128]{0:T(128)S(1)}) fusion(f32[]{:T(128)} %bitcast.337, f32[96,128]{1,0:T(8,128)} %bitcast.2580, f32[128]{0:T(128)S(1)} %get-tuple-element.457, f32[]{:T(128)} %bitcast.341, f32[]{:T(128)} %bitcast.339), kind=kLoop, calls=%fused_computation.1013 | loop fusion | flops 768 | bytes 3084 | tf_op jit(solution)/shard_map/broadcast_in_dim | solution.py:44
  122.4 2.8 %fusion.517 = (f32[1,128]{1,0:T(1,128)S(1)}, f32[128]{0:T(128)S(1)}) fusion(f32[]{:T(128)} %bitcast.333, f32[96,128]{1,0:T(8,128)} %bitcast.2581, f32[128]{0:T(128)S(1)} %get-tuple-element.459, f32[]{:T(128)} %bitcast.337, f32[]{:T(128)} %bitcast.335), kind=kLoop, calls=%fused_computation.1012 | loop fusion | flops 768 | bytes 3084 | tf_op jit(solution)/shard_map/broadcast_in_dim | solution.py:44
  125.2 2.7 %fusion.516 = (f32[1,128]{1,0:T(1,128)S(1)}, f32[128]{0:T(128)S(1)}) fusion(f32[]{:T(128)} %bitcast.329, f32[96,128]{1,0:T(8,128)} %bitcast.2582, f32[128]{0:T(128)S(1)} %get-tuple-element.461, f32[]{:T(128)} %bitcast.333, f32[]{:T(128)} %bitcast.331), kind=kLoop, calls=%fused_computation.1011 | loop fusion | flops 768 | bytes 3084 | tf_op jit(solution)/shard_map/broadcast_in_dim | solution.py:44
  137.3 5.8 %fusion.177 = f32[5,8,64,128]{3,2,1,0:T(8,128)S(1)} fusion(f32[5,8,64,2]{3,2,1,0:T(8,128)} %copy.10, f32[5,8,64,128]{3,2,1,0:T(8,128)S(1)} %copy-done, f32[5,8,64,2]{3,2,1,0:T(8,128)} %copy.8, f32[128,128]{1,0:T(8,128)S(1)} %concatenate.121), kind=kOutput, calls=%fused_computation.256 | convolution fusion | flops 506265600 | bytes 2727936 | tf_op jit(solution)/shard_map/ij,fatj->fati/dot_general | solution.py:99
  146.2 3.8 %collective-permute-start.6 = (f32[5,8,1,64]{3,1,0,2:T(8,128)S(1)}, f32[5,8,1,64]{3,1,0,2:T(8,128)S(1)}, u32[]{:S(2)}, u32[]{:S(2)}) collective-permute-start(f32[5,8,1,64]{3,1,0,2:T(8,128)S(1)} %bitcast.2593), channel_id=1, source_target_pairs={{0,8},{8,16},{16,24},{1,9},{9,17},{17,25},{2,10},{10,18},{18,26},{... | collective-permute-start | bytes 30728 | tf_op jit(solution)/shard_map/ppermute | solution.py:20
  156.8 4.0 %convolution_bitcast_fusion.1 = f32[5,8,64,128]{3,2,1,0:T(8,128)S(1)} fusion(f32[5,8,69,128]{3,2,1,0:T(8,128)} %constant_dynamic-update-slice_fusion, f32[5,8,64,128]{3,2,1,0:T(8,128)S(1)} %copy-done, f32[5,8,5,128]{3,2,1,0:T(8,128)} %collective-permute-done.1, f32[64,64]{1,0:T(8,128)S(1)} %concatenate.113), kind=kOutput, calls=%fused_computation.240 | convolution fusion | flops 253952000 | bytes 5423104 | tf_op jit(solution)/shard_map/ij,fajr->fair/dot_general | solution.py:75
  160.8 4.3 %convolution_bitcast_fusion = f32[5,8,64,128]{3,2,1,0:T(8,128)S(1)} fusion(f32[5,8,64,128]{3,2,1,0:T(8,128)S(1)} %copy-done, f32[5,8,5,128]{3,2,1,0:T(8,128)} %collective-permute-done.1, f32[5,8,69,128]{3,2,1,0:T(8,128)S(1)} %copy-done.1, f32[64,64]{1,0:T(8,128)S(1)} %concatenate.114), kind=kOutput, calls=%fused_computation.239 | convolution fusion | flops 258539520 | bytes 9310208 | tf_op jit(solution)/shard_map/ij,fajr->fair/dot_general | solution.py:76
  165.3 4.1 %collective-permute-start.3 = (f32[5,8,1,256]{3,2,1,0:T(1,128)S(1)}, f32[5,8,1,256]{3,2,1,0:T(1,128)S(1)}, u32[]{:S(2)}, u32[]{:S(2)}) collective-permute-start(f32[5,8,1,256]{3,2,1,0:T(1,128)S(1)} %get-tuple-element.750), channel_id=1, source_target_pairs={{1,0},{2,1},{3,2},{4,3},{5,4},{6,5},{7,6},{0,7},{9,8},{10,9},{11,1... | collective-permute-start | bytes 122888 | tf_op jit(solution)/shard_map/ppermute | solution.py:23
  (129 shorter events, 42.3 us)
Async XLA Ops:
  1.7 155.1 %collective-permute-start.1 = (f32[5,8,5,128]{3,2,1,0:T(8,128)S(1)}, f32[5,8,5,128]{3,2,1,0:T(8,128)}, u32[]{:S(2)}, u32[]{:S(2)}) collective-permute-start(f32[5,8,5,128]{3,2,1,0:T(8,128)S(1)} %get-tuple-element.741), channel_id=1, source_target_pairs={{0,1},{1,2},{2,3},{3,4},{4,5},{5,6},{6,7},{7,0},{8,9},{9,10},{10,1... | collective-permute-start | bytes 307208 | tf_op jit(solution)/shard_map/ppermute | solution.py:20
  3.8 152.3 %collective-permute-start = (f32[5,8,5,128]{3,2,1,0:T(8,128)S(1)}, f32[5,8,5,128]{3,2,1,0:T(8,128)S(1)}, u32[]{:S(2)}, u32[]{:S(2)}) collective-permute-start(f32[5,8,5,128]{3,2,1,0:T(8,128)S(1)} %get-tuple-element.742), channel_id=1, source_target_pairs={{1,0},{2,1},{3,2},{4,3},{5,4},{6,5},{7,6},{0,7},{9,8},{10,9},{11,1... | collective-permute-start | bytes 307208 | tf_op jit(solution)/shard_map/ppermute | solution.py:23
  9.6 126.2 %collective-permute-start.5 = (f32[5,8,64,2]{2,1,3,0:T(8,128)S(1)}, f32[5,8,64,2]{2,1,3,0:T(8,128)S(1)}, u32[]{:S(2)}, u32[]{:S(2)}) collective-permute-start(f32[5,8,64,2]{2,1,3,0:T(8,128)S(1)} %copy.15), channel_id=1, source_target_pairs={{0,8},{8,16},{16,24},{1,9},{9,17},{17,25},{2,10},{10,18},{18,26},{... | collective-permute-start | bytes 61448 | tf_op jit(solution)/shard_map/ppermute | solution.py:20
  13.8 10.4 %copy-start = (f32[5,8,64,128]{3,2,1,0:T(8,128)S(1)}, f32[5,8,64,128]{3,2,1,0:T(8,128)}, u32[]{:S(2)}) copy-start(f32[5,8,64,128]{3,2,1,0:T(8,128)} %param.19) | copy-start | bytes 3932164
  14.2 120.0 %collective-permute-start.4 = (f32[5,8,64,2]{2,1,3,0:T(8,128)S(1)}, f32[5,8,64,2]{2,1,3,0:T(8,128)S(1)}, u32[]{:S(2)}, u32[]{:S(2)}) collective-permute-start(f32[5,8,64,2]{2,1,3,0:T(8,128)S(1)} %copy.14), channel_id=1, source_target_pairs={{8,0},{16,8},{24,16},{9,1},{17,9},{25,17},{10,2},{18,10},{26,18},{... | collective-permute-start | bytes 61448 | tf_op jit(solution)/shard_map/ppermute | solution.py:23
  22.7 69.1 %copy-start.2 = (f32[3,32,128]{2,1,0:T(8,128)}, f32[3,32,128]{2,1,0:T(8,128)S(1)}, u32[]{:S(2)}) copy-start(f32[3,32,128]{2,1,0:T(8,128)S(1)} %get-tuple-element.336) | copy-start | bytes 147460
  144.3 11.7 %collective-permute-start.7 = (f32[5,8,1,64]{3,1,0,2:T(8,128)S(1)}, f32[5,8,1,64]{3,1,0,2:T(8,128)S(1)}, u32[]{:S(2)}, u32[]{:S(2)}) collective-permute-start(f32[5,8,1,64]{3,1,0,2:T(8,128)S(1)} %bitcast.2595), channel_id=1, source_target_pairs={{8,0},{16,8},{24,16},{9,1},{17,9},{25,17},{10,2},{18,10},{26,18},{... | collective-permute-start | bytes 30728 | tf_op jit(solution)/shard_map/ppermute | solution.py:23
  146.2 9.8 %collective-permute-start.6 = (f32[5,8,1,64]{3,1,0,2:T(8,128)S(1)}, f32[5,8,1,64]{3,1,0,2:T(8,128)S(1)}, u32[]{:S(2)}, u32[]{:S(2)}) collective-permute-start(f32[5,8,1,64]{3,1,0,2:T(8,128)S(1)} %bitcast.2593), channel_id=1, source_target_pairs={{0,8},{8,16},{16,24},{1,9},{9,17},{17,25},{2,10},{10,18},{18,26},{... | collective-permute-start | bytes 30728 | tf_op jit(solution)/shard_map/ppermute | solution.py:20
  156.8 4.0 %copy-start.1 = (f32[5,8,69,128]{3,2,1,0:T(8,128)S(1)}, f32[5,8,69,128]{3,2,1,0:T(8,128)}, u32[]{:S(2)}) copy-start(f32[5,8,69,128]{3,2,1,0:T(8,128)} %constant_dynamic-update-slice_fusion) | copy-start | bytes 4239364
  160.8 8.7 %copy-start.3 = (f32[128]{0:T(128)S(1)}, f32[128]{0:T(128)}, u32[]{:S(2)}) copy-start(f32[128]{0:T(128)} %param.20) | copy-start | bytes 1540
  165.3 5.9 %collective-permute-start.2 = (f32[5,8,1,256]{3,2,1,0:T(1,128)S(1)}, f32[5,8,1,256]{3,2,1,0:T(1,128)S(1)}, u32[]{:S(2)}, u32[]{:S(2)}) collective-permute-start(f32[5,8,1,256]{3,2,1,0:T(1,128)S(1)} %get-tuple-element.749), channel_id=1, source_target_pairs={{0,1},{1,2},{2,3},{3,4},{4,5},{5,6},{6,7},{7,0},{8,9},{9,10},{10,1... | collective-permute-start | bytes 122888 | tf_op jit(solution)/shard_map/ppermute | solution.py:20
  165.3 5.8 %collective-permute-start.3 = (f32[5,8,1,256]{3,2,1,0:T(1,128)S(1)}, f32[5,8,1,256]{3,2,1,0:T(1,128)S(1)}, u32[]{:S(2)}, u32[]{:S(2)}) collective-permute-start(f32[5,8,1,256]{3,2,1,0:T(1,128)S(1)} %get-tuple-element.750), channel_id=1, source_target_pairs={{1,0},{2,1},{3,2},{4,3},{5,4},{6,5},{7,6},{0,7},{9,8},{10,9},{11,1... | collective-permute-start | bytes 122888 | tf_op jit(solution)/shard_map/ppermute | solution.py:23
  171.5 1.4 copy-start.4
where the time goes:
time: 176 us; the launch traced here: 174 us
  other arithmetic  108 us (61%)
  starting transfers between devices  21.2 us (12%)
  local copies, waits for them, and re-layouts  20.6 us (12%)
  matrix products  14.1 us (8%)
  between operations  6.38 us (4%)
  loops' own time  4.31 us (2%)
    sub x5, other arithmetic, local_tables(): lax.linalg.tridiagonal_solve(lower, middle, upper, jnp.eye(cells, dtype=j...  60.2 us
    broadcast_in_dim x36, other arithmetic, local_tables(): lax.linalg.tridiagonal_solve(lower, middle, upper, jnp.eye(cells, dtype=j...  41.5 us
    ppermute x4, starting transfers between devices, extended(): lax.ppermute(lax.slice_in_dim(block, 0, width, axis=dim), axis, backward)  11.1 us
    ppermute x4, starting transfers between devices, extended(): lax.ppermute(lax.slice_in_dim(block, block.shape[dim] - width, None, axis...  10.1 us
    dot_general x1, matrix products, local(): jnp.einsum('ij,fatj->fati', radial_inv, radial_side, precision=HIGHEST)  5.83 us
    slice x11, local copies, waits for them, and re-layouts, local_tables(): lax.linalg.tridiagonal_solve(lower, middle, upper, jnp.eye(cells, dtype=j...  5.83 us
    another operation x2, loops' own time, local_tables(): lax.linalg.tridiagonal_solve(lower, middle, upper, jnp.eye(cells, dtype=j...  4.31 us
    dot_general x1, matrix products, local(): jnp.einsum('ij,fajr->fair', smooth_inv, smooth_side, precision=HIGHEST)  4.25 us
  transfers between devices with their start and end apart: 8, of which 0 were waited for; matrix products, arithmetic and copies ran while one was open for 74% of the time, Pallas kernels for 0%

commit v1 on v0

v1 whole, which is shorter than its diff:
```python
import functools

import jax
import jax.numpy as jnp
import ml_dtypes
import numpy as np
from jax import lax
from jax.experimental import pallas as pl
from jax.experimental.pallas import tpu as pltpu
from jax.sharding import PartitionSpec as P

ALPHA_D = 1.0 / 3.0
COEF_A = 14.0 / 9.0
COEF_B = 1.0 / 9.0
ALPHA_F = 0.49
MESH = pl.DeviceIdType.MESH
BF16 = jnp.bfloat16
F32 = jnp.float32

EDGE = 6
PACK = 4


def filter_weights():
    slack = 1.0 - 2.0 * ALPHA_F
    return [
        (193.0 + 126.0 * ALPHA_F) / 256.0,
        (105.0 + 302.0 * ALPHA_F) / 256.0,
        -15.0 * slack / 64.0,
        45.0 * slack / 512.0,
        -5.0 * slack / 256.0,
        slack / 512.0,
    ]


def split(table):
    table = np.asarray(table, np.float32)
    high = table.astype(ml_dtypes.bfloat16)
    low = (table - high.astype(np.float32)).astype(ml_dtypes.bfloat16)
    return high, low


def decay(alpha):
    return (-1.0 + np.sqrt(1.0 - 4.0 * alpha * alpha)) / (2.0 * alpha)


def azimuth_tables(cells, blocks):
    total = cells * blocks
    wave = 2.0 * np.pi * np.arange(total) / total
    slope_symbol = 1j * (COEF_A * np.sin(wave) + 0.5 * COEF_B * np.sin(2.0 * wave))
    slope_symbol = slope_symbol / (1.0 + 2.0 * ALPHA_D * np.cos(wave))
    weights = filter_weights()
    smooth_symbol = sum(w * np.cos(n * wave) for n, w in enumerate(weights))
    smooth_symbol = smooth_symbol / (1.0 + 2.0 * ALPHA_F * np.cos(wave))
    slope = np.real(np.fft.ifft(slope_symbol))
    smooth = np.real(np.fft.ifft(smooth_symbol))
    i = np.arange(cells)
    gap = (i[:, None] - i[None, :]) % total
    main = np.concatenate([slope[gap], smooth[gap]], axis=0)
    rate_d, rate_f = decay(ALPHA_D), decay(ALPHA_F)
    scale_d = slope[2] / rate_d**2
    scale_f = smooth[5] / rate_f**5
    send_right = np.zeros((EDGE, cells))
    send_right[0] = rate_d ** (cells - 1 - i)
    send_right[1] = rate_f ** (cells - 1 - i)
    use_left = np.zeros((2 * cells, EDGE))
    use_left[:cells, 0] = scale_d * rate_d ** (i + 1)
    use_left[cells:, 1] = scale_f * rate_f ** (i + 1)
    for m in range(EDGE - 2):
        send_right[2 + m, cells - 1 - m] = 1.0
        for row in range(EDGE - 2 - m):
            n = row + 1 + m
            if n < 2:
                use_left[row, 2 + m] = slope[n] - scale_d * rate_d**n
            if n < 5:
                use_left[cells + row, 2 + m] = smooth[n] - scale_f * rate_f**n
    send_left = send_right[:, ::-1]
    use_right = np.concatenate([-use_left[:cells][::-1], use_left[cells:][::-1]], axis=0)
    return main, send_right, send_left, use_left, use_right


def radial_matrix(total):
    system = np.eye(total) + ALPHA_D * (np.eye(total, k=1) + np.eye(total, k=-1))
    side = 0.5 * COEF_A * (np.eye(total, k=1) - np.eye(total, k=-1))
    side = side + 0.25 * COEF_B * (np.eye(total, k=2) - np.eye(total, k=-2))
    return np.linalg.solve(system, side)


def rank_two(corner):
    cells = corner.shape[0]
    send = np.zeros((2, cells))
    send[0] = corner[1] / corner[1, cells - 1]
    send[1, cells - 1] = 1.0
    use = np.zeros((cells, 2))
    use[1:, 0] = corner[1:, cells - 1]
    use[0, 0] = corner[0, cells - 2] / send[0, cells - 2]
    use[0, 1] = corner[0, cells - 1] - use[0, 0]
    return use, send


def radial_tables(cells, blocks):
    full = radial_matrix(cells * blocks).reshape(blocks, cells, blocks, cells)
    main = np.stack([full[b, :, b, :] for b in range(blocks)])
    use_left = np.zeros((blocks, cells, 2))
    use_right = np.zeros((blocks, cells, 2))
    send_right = np.zeros((blocks, 2, cells))
    send_left = np.zeros((blocks, 2, cells))
    for b in range(1, blocks):
        use_left[b], send_right[b - 1] = rank_two(full[b, :, b - 1, :])
    for b in range(blocks - 1):
        use, send = rank_two(full[b, :, b + 1, :][::-1, ::-1])
        use_right[b], send_left[b + 1] = use[::-1], send[:, ::-1]
    return main, send_right, send_left, use_left, use_right


def build_tables(cells_t, azi_count, cells_r, rad_count):
    main, send_right, send_left, use_left, use_right = azimuth_tables(cells_t, azi_count)
    sends = np.zeros((16, cells_t))
    sends[:EDGE], sends[8 : 8 + EDGE] = send_right, send_left
    high, low = split(sends)
    azi_send = np.concatenate([high, low, high], axis=1)
    uses = np.zeros((2 * cells_t, 16))
    uses[:, :EDGE], uses[:, 8 : 8 + EDGE] = use_left, use_right
    high, low = split(main)
    use_high, use_low = split(uses)
    azi_main = np.concatenate([high, low, high, use_high, use_low, use_high], axis=1)

    main, send_right, send_left, use_left, use_right = radial_tables(cells_r, rad_count)
    sends = np.concatenate([send_right, send_left], axis=1)
    high, low = split(sends)
    rad_send = np.zeros((rad_count, 16, 2 * cells_r), ml_dtypes.bfloat16)
    rad_send[:, 0:4, :cells_r] = high
    rad_send[:, 0:4, cells_r:] = high
    rad_send[:, 8:12, :cells_r] = low
    turned = np.swapaxes(main, 1, 2)
    high, low = split(turned)
    rad_main = np.zeros((rad_count, 2 * cells_r, 2 * cells_r), ml_dtypes.bfloat16)
    rad_main[:, :cells_r, :cells_r] = high
    rad_main[:, :cells_r, cells_r:] = low
    rad_main[:, cells_r:, :cells_r] = high
    uses = np.swapaxes(np.concatenate([use_left, use_right], axis=2), 1, 2)
    high, low = split(uses)
    rad_use = np.zeros((rad_count, 16, cells_r), ml_dtypes.bfloat16)
    rad_use[:, 0:4], rad_use[:, 4:8], rad_use[:, 8:12] = high, low, high
    return azi_send, azi_main, rad_send, rad_main, rad_use


def halves(x):
    high = x.astype(BF16)
    return high, (x - high.astype(F32)).astype(BF16)


def dot(a, b):
    return jnp.dot(a, b, preferred_element_type=F32)


def exchange_kernel(
    azi_count, rad_count, chunk,
    fields, azi_send, rad_send,
    from_left, from_right, from_in, from_out,
    block, to_right, to_left, to_out, to_in, load_sem, send_sem, recv_sem,
):
    planes, cells_t, cells_r = block.shape
    rad, azi = lax.axis_index("rad"), lax.axis_index("azi")
    right = (rad, lax.rem(azi + 1, azi_count))
    left = (rad, lax.rem(azi + azi_count - 1, azi_count))
    outer = (lax.rem(rad + 1, rad_count), azi)
    inner = (lax.rem(rad + rad_count - 1, rad_count), azi)
    barrier = pltpu.get_barrier_semaphore()
    for place in (right, left, outer, inner):
        pl.semaphore_signal(barrier, inc=1, device_id=place, device_id_type=MESH)
    count = planes // chunk
    loads = []
    for c in range(count):
        span = pl.ds(c * chunk, chunk)
        load = pltpu.make_async_copy(fields.at[span], block.at[span], load_sem.at[c])
        load.start()
        loads.append(load)
    radial_weights = rad_send[rad]
    for c in range(count):
        loads[c].wait()
        rows = chunk * cells_t
        high, low = halves(block[pl.ds(c * chunk, chunk)])
        pairs = jnp.concatenate([high.reshape(rows, cells_r), low.reshape(rows, cells_r)], axis=1)
        ends = lax.dot_general(
            radial_weights, pairs, (((1,), (1,)), ((), ())), preferred_element_type=F32
        )
        ends = ends[0:8] + ends[8:16]
        to_out[:, c * rows : (c + 1) * rows] = ends[0:2]
        to_in[:, c * rows : (c + 1) * rows] = ends[2:4]
        for p in range(chunk):
            stack = jnp.concatenate([high[p], high[p], low[p]], axis=0)
            edge = dot(azi_send[...], stack)
            group, slot = divmod(c * chunk + p, PACK)
            to_right[group, EDGE * slot : EDGE * (slot + 1), :] = edge[0:EDGE]
            to_left[group, EDGE * slot : EDGE * (slot + 1), :] = edge[8 : 8 + EDGE]
    pl.semaphore_wait(barrier, 4)
    copies = []
    for k, (source, target, place) in enumerate(
        (
            (to_right, from_left, right),
            (to_left, from_right, left),
            (to_out, from_in, outer),
            (to_in, from_out, inner),
        )
    ):
        copy = pltpu.make_async_remote_copy(
            src_ref=source,
            dst_ref=target,
            send_sem=send_sem.at[k],
            recv_sem=recv_sem.at[k],
            device_id=place,
            device_id_type=MESH,
        )
        copy.start()
        copies.append(copy)
    for copy in copies:
        copy.wait()


def solve_kernel(
    fields, from_left, from_right, from_in, from_out, azi_main, rad_main, rad_use,
    azimuth_metric, radial_metric,
    grad_azimuth, grad_radial, filtered,
    rims, ends,
):
    planes, cells_t, cells_r = fields.shape
    rad = lax.axis_index("rad")
    rows = planes * cells_t

    rims[...] = jnp.zeros_like(rims)
    ends[...] = jnp.zeros_like(ends)
    ends[0:2] = from_in[...]
    ends[2:4] = from_out[...]
    rim = ends[0:4]
    rim_high = rim.astype(BF16).astype(F32)
    ends[0:4] = rim_high
    ends[4:8] = rim_high
    ends[8:12] = rim - rim_high
    radial_rim = lax.dot_general(
        ends[...].astype(BF16), rad_use[rad], (((0,), (0,)), ((), ())), preferred_element_type=F32
    )
    high, low = halves(fields[...])
    pairs = jnp.concatenate([high.reshape(rows, cells_r), low.reshape(rows, cells_r)], axis=1)
    both = dot(pairs, rad_main[rad])
    slope = (both[:, :cells_r] + both[:, cells_r:] + radial_rim) * radial_metric[...]
    grad_radial[...] = slope.reshape(planes, cells_t, cells_r)
    for p in range(planes):
        group, slot = divmod(p, PACK)
        rims[p, 0:EDGE, :] = from_left[group, EDGE * slot : EDGE * (slot + 1), :]
        rims[p, 8 : 8 + EDGE, :] = from_right[group, EDGE * slot : EDGE * (slot + 1), :]
    for p in range(0, planes, 2):
        stacks = []
        for q in (p, p + 1):
            rim_h, rim_l = halves(rims[q])
            stacks.append(
                jnp.concatenate([high[q], high[q], low[q], rim_h, rim_h, rim_l], axis=0)
            )
        result = dot(azi_main[...], jnp.concatenate(stacks, axis=1))
        for k, q in enumerate((p, p + 1)):
            lanes = slice(k * cells_r, (k + 1) * cells_r)
            grad_azimuth[q] = result[:cells_t, lanes] * azimuth_metric[...]
            filtered[q] = result[cells_t:, lanes]


def local(tables, azi_count, rad_count, fields, radial_metric, azimuth_metric):
    azi_send, azi_main, rad_send, rad_main, rad_use = [jnp.asarray(t) for t in tables]
    shape = fields.shape
    cells_t, cells_r = shape[2], shape[3]
    planes = shape[0] * shape[1]
    x = fields.reshape(planes, cells_t, cells_r)
    chunk = 8
    steps = planes // chunk
    rims = jax.ShapeDtypeStruct((planes // PACK, PACK * EDGE, cells_r), F32)
    ends = jax.ShapeDtypeStruct((2, planes * cells_t), F32)
    hbm = pl.BlockSpec(memory_space=pl.ANY)
    vmem = pl.BlockSpec(memory_space=pltpu.VMEM)
    from_left, from_right, from_in, from_out = pl.pallas_call(
        functools.partial(exchange_kernel, azi_count, rad_count, chunk),
        out_shape=[rims, rims, ends, ends],
        in_specs=[hbm, vmem, vmem],
        out_specs=[hbm] * 4,
        scratch_shapes=[
            pltpu.VMEM(x.shape, F32),
            pltpu.VMEM(rims.shape, F32),
            pltpu.VMEM(rims.shape, F32),
            pltpu.VMEM(ends.shape, F32),
            pltpu.VMEM(ends.shape, F32),
            pltpu.SemaphoreType.DMA((steps,)),
            pltpu.SemaphoreType.DMA((4,)),
            pltpu.SemaphoreType.DMA((4,)),
        ],
        compiler_params=pltpu.CompilerParams(
            collective_id=0, has_side_effects=True, vmem_limit_bytes=32 * 2**20
        ),
    )(x, azi_send, rad_send)

    def whole(a):
        return pl.BlockSpec(a.shape, lambda i: (0,) * a.ndim)

    part = pl.BlockSpec((chunk, cells_t, cells_r), lambda i: (i, 0, 0))
    rim_part = pl.BlockSpec((chunk // PACK, PACK * EDGE, cells_r), lambda i: (i, 0, 0))
    end_part = pl.BlockSpec((2, chunk * cells_t), lambda i: (0, i))
    metrics = (azimuth_metric.reshape(1, cells_r), radial_metric.reshape(1, cells_r))
    outs = pl.pallas_call(
        solve_kernel,
        grid=(steps,),
        out_shape=[jax.ShapeDtypeStruct(x.shape, F32)] * 3,
        in_specs=[part, rim_part, rim_part, end_part, end_part]
        + [whole(a) for a in (azi_main, rad_main, rad_use) + metrics],
        out_specs=[part] * 3,
        scratch_shapes=[
            pltpu.VMEM((chunk, 16, cells_r), F32),
            pltpu.VMEM((16, chunk * cells_t), F32),
        ],
        compiler_params=pltpu.CompilerParams(vmem_limit_bytes=32 * 2**20),
    )(x, from_left, from_right, from_in, from_out, azi_main, rad_main, rad_use, *metrics)
    return tuple(a.reshape(shape) for a in outs)


def solution(mesh):
    rad_count, azi_count = mesh.shape["rad"], mesh.shape["azi"]
    spec = P(None, None, "azi", "rad")

    def run(fields, radial_metric, azimuth_metric):
        tables = build_tables(
            fields.shape[2] // azi_count, azi_count, fields.shape[3] // rad_count, rad_count
        )
        body = functools.partial(local, tables, azi_count, rad_count)
        return jax.shard_map(
            body,
            mesh=mesh,
            in_specs=(spec, P("rad"), P("rad")),
            out_specs=(spec, spec, spec),
            check_vma=False,
        )(fields, radial_metric, azimuth_metric)

    return run
```

time: 176 us -> 18.6 us (0.11)
  the two profiles are of different devices: /device:TPU:1 before, /device:TPU:0 now
where the time goes in v1:
time: 18.6 us; the launch traced here: 18.3 us
  Pallas kernels  14.8 us (80%)
  local copies, waits for them, and re-layouts  2.79 us (15%)
  between operations  0.71 us (4%)
    pallas_call x1, Pallas kernels, local(): pl.pallas_call(functools.partial(exchange_kernel, azi_count, rad_count, c...  11.2 us
    pallas_call x1, Pallas kernels, local(): pl.pallas_call(solve_kernel, grid=(steps,), out_shape=[jax.ShapeDtypeStru...  3.62 us
    unnamed x16, local copies, waits for them, and re-layouts  2.79 us

profile of v1, /device:TPU:0, one launch (start us, length us, event | category | flops | bytes accessed | tf_op | source)
XLA Modules:
  0.0 18.3 jit_solution(489241127200784117)
XLA Ops:
  0.6 0.0 copy-start.6
  0.6 0.0 copy-start.7
  0.7 0.0 copy-start
  0.7 1.3 %copy-done = f32[5,8,64,128]{3,2,1,0:T(8,128)S(1)} copy-done((f32[5,8,64,128]{3,2,1,0:T(8,128)S(1)}, f32[5,8,64,128]{3,2,1,0:T(8,128)}, u32[]{:S(2)}) %copy-start) | copy-done | bytes 1310744
  2.0 0.0 copy-start.3
  2.0 0.8 %copy-done.3 = bf16[4,16,256]{2,1,0:T(8,128)(2,1)S(1)} copy-done((bf16[4,16,256]{2,1,0:T(8,128)(2,1)S(1)}, bf16[4,16,256]{2,1,0:T(8,128)(2,1)}, u32[]{:S(2)}) %copy-start.3) | copy-done | bytes 32792
  2.7 0.0 copy-start.5
  2.7 0.7 %copy-done.5 = bf16[16,192]{1,0:T(8,128)(2,1)S(1)} copy-done((bf16[16,192]{1,0:T(8,128)(2,1)S(1)}, bf16[16,192]{1,0:T(8,128)(2,1)}, u32[]{:S(2)}) %copy-start.5) | copy-done | bytes 6168
  3.4 0.0 copy-start.1
  3.4 0.0 copy-start.2
  3.4 0.0 copy-start.4
  3.4 11.2 %shard_map.103 = (f32[10,24,128]{2,1,0:T(8,128)S(1)}, f32[10,24,128]{2,1,0:T(8,128)S(1)}, f32[2,2560]{1,0:T(2,128)S(1)}, f32[2,2560]{1,0:T(2,128)S(1)}) custom-call(f32[40,64,128]{2,1,0:T(8,128)S(1)} %bitcast.6, bf16[16,192]{1,0:T(8,128)(2,1)S(1)} %copy-done.5, bf16[4,16,256]{2,1,0:T(8,128)(2,1)S(1)} %copy-done.3), custom_call_target="tpu_custom_call" | custom-call | tf_op jit(solution)/shard_map/pallas_call | solution.py:278
  14.7 0.0 copy-done.6
  14.7 0.0 copy-done.7
  14.7 0.0 copy-done.1
  14.7 0.0 copy-done.2
  14.7 0.0 copy-done.4
  14.7 3.6 %shard_map.104 = (f32[40,64,128]{2,1,0:T(8,128)}, f32[40,64,128]{2,1,0:T(8,128)}, f32[40,64,128]{2,1,0:T(8,128)}) custom-call(f32[40,64,128]{2,1,0:T(8,128)S(1)} %bitcast.7, f32[10,24,128]{2,1,0:T(8,128)S(1)} %get-tuple-element.10.from_left, f32[10,24,128]{2,1,0:T(8,128)S(1)} %get-tuple-element.11.from_right, f32[2,2560]{1,0:T(2,128)S(1)} %get-tuple-element.12.from_in, ...), custom_call_target="tpu_custom_call" | custom-call | tf_op jit(solution)/shard_map/pallas_call | solution.py:305
Async XLA Ops:
  0.6 14.0 %copy-start.6 = (f32[128]{0:T(128)S(1)}, f32[128]{0:T(128)}, u32[]{:S(2)}) copy-start(f32[128]{0:T(128)} %param.10) | copy-start | bytes 1540
  0.6 14.0 %copy-start.7 = (f32[128]{0:T(128)S(1)}, f32[128]{0:T(128)}, u32[]{:S(2)}) copy-start(f32[128]{0:T(128)} %param.9) | copy-start | bytes 1540
  0.7 1.3 %copy-start = (f32[5,8,64,128]{3,2,1,0:T(8,128)S(1)}, f32[5,8,64,128]{3,2,1,0:T(8,128)}, u32[]{:S(2)}) copy-start(f32[5,8,64,128]{3,2,1,0:T(8,128)} %param.8) | copy-start | bytes 3932164
  2.0 0.8 %copy-start.3 = (bf16[4,16,256]{2,1,0:T(8,128)(2,1)S(1)}, bf16[4,16,256]{2,1,0:T(8,128)(2,1)}, u32[]{:S(2)}) copy-start(bf16[4,16,256]{2,1,0:T(8,128)(2,1)} %constant.12.clone.rad_send) | copy-start | bytes 98308
  2.7 0.7 %copy-start.5 = (bf16[16,192]{1,0:T(8,128)(2,1)S(1)}, bf16[16,192]{1,0:T(8,128)(2,1)}, u32[]{:S(2)}) copy-start(bf16[16,192]{1,0:T(8,128)(2,1)} %constant.10.clone.azi_send) | copy-start | bytes 18436
  3.4 11.3 %copy-start.1 = (bf16[4,256,256]{2,1,0:T(8,128)(2,1)S(1)}, bf16[4,256,256]{2,1,0:T(8,128)(2,1)}, u32[]{:S(2)}) copy-start(bf16[4,256,256]{2,1,0:T(8,128)(2,1)} %constant.13.clone.rad_main) | copy-start | bytes 1572868
  3.4 11.3 %copy-start.2 = (bf16[128,240]{1,0:T(8,128)(2,1)S(1)}, bf16[128,240]{1,0:T(8,128)(2,1)}, u32[]{:S(2)}) copy-start(bf16[128,240]{1,0:T(8,128)(2,1)} %constant.11.clone.azi_main) | copy-start | bytes 184324
  3.4 11.3 %copy-start.4 = (bf16[4,16,128]{2,1,0:T(8,128)(2,1)S(1)}, bf16[4,16,128]{2,1,0:T(8,128)(2,1)}, u32[]{:S(2)}) copy-start(bf16[4,16,128]{2,1,0:T(8,128)(2,1)} %constant.14.clone.rad_use) | copy-start | bytes 49156

commit v2 on v1

--- a/solution.py
+++ b/solution.py
@@ -123,7 +123,8 @@
     uses[:, :EDGE], uses[:, 8 : 8 + EDGE] = use_left, use_right
     high, low = split(main)
     use_high, use_low = split(uses)
-    azi_main = np.concatenate([high, low, high, use_high, use_low, use_high], axis=1)
+    azi_main = np.concatenate([high, low, high], axis=1)
+    azi_use = np.concatenate([use_high, use_low, use_high], axis=1)
 
     main, send_right, send_left, use_left, use_right = radial_tables(cells_r, rad_count)
     sends = np.concatenate([send_right, send_left], axis=1)
@@ -142,7 +143,7 @@
     high, low = split(uses)
     rad_use = np.zeros((rad_count, 16, cells_r), ml_dtypes.bfloat16)
     rad_use[:, 0:4], rad_use[:, 4:8], rad_use[:, 8:12] = high, low, high
-    return azi_send, azi_main, rad_send, rad_main, rad_use
+    return azi_send, azi_main, azi_use, rad_send, rad_main, rad_use
 
 
 def halves(x):
@@ -154,13 +155,18 @@
     return jnp.dot(a, b, preferred_element_type=F32)
 
 
-def exchange_kernel(
+def block_kernel(
     azi_count, rad_count, chunk,
-    fields, azi_send, rad_send,
-    from_left, from_right, from_in, from_out,
-    block, to_right, to_left, to_out, to_in, load_sem, send_sem, recv_sem,
+    fields, azi_send, azi_main, rad_send, rad_main, rad_use, radial_metric,
+    from_left, from_right, part_slope, part_smooth, grad_radial,
+    block, azi_send_v, azi_main_v, rad_send_v, rad_main_v, rad_use_v, metric,
+    to_right, to_left, to_out, to_in, from_in, from_out, ends,
+    table_sem, load_sem, send_sem, recv_sem, rad_send_sem, rad_recv_sem,
 ):
     planes, cells_t, cells_r = block.shape
+    count = planes // chunk
+    rows = chunk * cells_t
+    groups = chunk // PACK
     rad, azi = lax.axis_index("rad"), lax.axis_index("azi")
     right = (rad, lax.rem(azi + 1, azi_count))
     left = (rad, lax.rem(azi + azi_count - 1, azi_count))
@@ -169,153 +175,255 @@
     barrier = pltpu.get_barrier_semaphore()
     for place in (right, left, outer, inner):
         pl.semaphore_signal(barrier, inc=1, device_id=place, device_id_type=MESH)
-    count = planes // chunk
-    loads = []
+
+    def load(c):
+        span = pl.ds(c * chunk, chunk)
+        return pltpu.make_async_copy(fields.at[span], block.at[span], load_sem.at[c])
+
+    tables = [
+        pltpu.make_async_copy(source, target, table_sem.at[k])
+        for k, (source, target) in enumerate(
+            (
+                (azi_send, azi_send_v),
+                (rad_send.at[rad], rad_send_v),
+                (azi_main, azi_main_v),
+                (rad_main.at[rad], rad_main_v),
+                (rad_use.at[rad], rad_use_v),
+                (radial_metric, metric),
+            )
+        )
+    ]
+    tables[0].start()
+    tables[1].start()
     for c in range(count):
-        span = pl.ds(c * chunk, chunk)
-        load = pltpu.make_async_copy(fields.at[span], block.at[span], load_sem.at[c])
-        load.start()
-        loads.append(load)
-    radial_weights = rad_send[rad]
-    for c in range(count):
-        loads[c].wait()
-        rows = chunk * cells_t
+        load(c).start()
+    for table in tables[2:]:
+        table.start()
+    tables[0].wait()
+    tables[1].wait()
+
+    def sends(c):
+        span = pl.ds(c * groups, groups)
+        return [
+            pltpu.make_async_remote_copy(
+                src_ref=source.at[span],
+                dst_ref=target.at[span],
+                send_sem=send_sem.at[k, c],
+                recv_sem=recv_sem.at[k, c],
+                device_id=place,
+                device_id_type=MESH,
+            )
+            for k, (source, target, place) in enumerate(
+                ((to_right, from_left, right), (to_left, from_right, left))
+            )
+        ]
+
+    def edges(c):
+        load(c).wait()
         high, low = halves(block[pl.ds(c * chunk, chunk)])
-        pairs = jnp.concatenate([high.reshape(rows, cells_r), low.reshape(rows, cells_r)], axis=1)
-        ends = lax.dot_general(
-            radial_weights, pairs, (((1,), (1,)), ((), ())), preferred_element_type=F32
-        )
-        ends = ends[0:8] + ends[8:16]
-        to_out[:, c * rows : (c + 1) * rows] = ends[0:2]
-        to_in[:, c * rows : (c + 1) * rows] = ends[2:4]
-        for p in range(chunk):
-            stack = jnp.concatenate([high[p], high[p], low[p]], axis=0)
-            edge = dot(azi_send[...], stack)
-            group, slot = divmod(c * chunk + p, PACK)
-            to_right[group, EDGE * slot : EDGE * (slot + 1), :] = edge[0:EDGE]
-            to_left[group, EDGE * slot : EDGE * (slot + 1), :] = edge[8 : 8 + EDGE]
+        for p in range(0, chunk, 2):
+            edge = dot(azi_send_v[...], stacked(high, low, p))
+            for k in range(2):
+                group, slot = divmod(p + k, PACK)
+                lanes = slice(k * cells_r, (k + 1) * cells_r)
+                span = slice(EDGE * slot, EDGE * (slot + 1))
+                to_right[c * groups + group, span, :] = edge[0:EDGE, lanes]
+                to_left[c * groups + group, span, :] = edge[8 : 8 + EDGE, lanes]
+
+    def radial_edges(c):
+        high, low = halves(block[pl.ds(c * chunk, chunk)])
+        tips = lax.dot_general(
+            rad_send_v[...], paired(high, low), (((1,), (1,)), ((), ())),
+            preferred_element_type=F32,
+        )
+        tips = tips[0:8] + tips[8:16]
+        span = pl.ds(pl.multiple_of(c * rows, rows), rows)
+        to_out[:, span] = tips[0:2]
+        to_in[:, span] = tips[2:4]
+
+    edges(0)
     pl.semaphore_wait(barrier, 4)
-    copies = []
-    for k, (source, target, place) in enumerate(
-        (
-            (to_right, from_left, right),
-            (to_left, from_right, left),
-            (to_out, from_in, outer),
-            (to_in, from_out, inner),
-        )
-    ):
-        copy = pltpu.make_async_remote_copy(
+    for copy in sends(0):
+        copy.start()
+
+    @pl.loop(1, count)
+    def _(c):
+        edges(c)
+        for copy in sends(c):
+            copy.start()
+
+    @pl.loop(0, count)
+    def _(c):
+        radial_edges(c)
+
+    radial_copies = [
+        pltpu.make_async_remote_copy(
             src_ref=source,
             dst_ref=target,
-            send_sem=send_sem.at[k],
-            recv_sem=recv_sem.at[k],
+            send_sem=rad_send_sem.at[k],
+            recv_sem=rad_recv_sem.at[k],
             device_id=place,
             device_id_type=MESH,
         )
+        for k, (source, target, place) in enumerate(
+            ((to_out, from_in, outer), (to_in, from_out, inner))
+        )
+    ]
+    for copy in radial_copies:
         copy.start()
-        copies.append(copy)
-    for copy in copies:
+    for table in tables[2:]:
+        table.wait()
+    ends[...] = jnp.zeros_like(ends)
+
+    @pl.loop(0, count)
+    def _(c):
+        high, low = halves(block[pl.ds(c * chunk, chunk)])
+        for p in range(0, chunk, 2):
+            result = dot(azi_main_v[...], stacked(high, low, p))
+            for k in range(2):
+                lanes = slice(k * cells_r, (k + 1) * cells_r)
+                part_slope[c * chunk + p + k] = result[:cells_t, lanes]
+                part_smooth[c * chunk + p + k] = result[cells_t:, lanes]
+
+    for copy in radial_copies:
         copy.wait()
 
-
-def solve_kernel(
-    fields, from_left, from_right, from_in, from_out, azi_main, rad_main, rad_use,
-    azimuth_metric, radial_metric,
-    grad_azimuth, grad_radial, filtered,
-    rims, ends,
+    @pl.loop(0, count)
+    def _(c):
+        span = pl.ds(pl.multiple_of(c * rows, rows), rows)
+        ends[0:2] = from_in[:, span]
+        ends[2:4] = from_out[:, span]
+        rim = ends[0:4]
+        rim_high = rim.astype(BF16).astype(F32)
+        ends[0:4] = rim_high
+        ends[4:8] = rim_high
+        ends[8:12] = rim - rim_high
+        high, low = halves(block[pl.ds(c * chunk, chunk)])
+        both = dot(paired(high, low), rad_main_v[...])
+        outside = lax.dot_general(
+            ends[...].astype(BF16), rad_use_v[...], (((0,), (0,)), ((), ())),
+            preferred_element_type=F32,
+        )
+        slope = (both[:, :cells_r] + both[:, cells_r:] + outside) * metric[...]
+        grad_radial[pl.ds(c * chunk, chunk)] = slope.reshape(chunk, cells_t, cells_r)
+
+    @pl.loop(0, count)
+    def _(c):
+        for copy in sends(c):
+            copy.wait()
+
+
+def stacked(high, low, p):
+    return jnp.concatenate(
+        [jnp.concatenate([high[q], high[q], low[q]], axis=0) for q in (p, p + 1)], axis=1
+    )
+
+
+def paired(high, low):
+    planes, cells_t, cells_r = high.shape
+    rows = planes * cells_t
+    return jnp.concatenate([high.reshape(rows, cells_r), low.reshape(rows, cells_r)], axis=1)
+
+
+def join_kernel(
+    chunk, part_slope, part_smooth, radial, from_left, from_right, azi_use, azimuth_metric,
+    grad_azimuth, filtered, grad_radial,
+    rims, sem,
 ):
-    planes, cells_t, cells_r = fields.shape
-    rad = lax.axis_index("rad")
-    rows = planes * cells_t
+    cells_t, cells_r = part_slope.shape[1:]
+    step = pl.program_id(0)
+    copy = pltpu.make_async_copy(radial, grad_radial, sem)
+
+    @pl.when(step == 0)
+    def _():
+        copy.start()
 
     rims[...] = jnp.zeros_like(rims)
-    ends[...] = jnp.zeros_like(ends)
-    ends[0:2] = from_in[...]
-    ends[2:4] = from_out[...]
-    rim = ends[0:4]
-    rim_high = rim.astype(BF16).astype(F32)
-    ends[0:4] = rim_high
-    ends[4:8] = rim_high
-    ends[8:12] = rim - rim_high
-    radial_rim = lax.dot_general(
-        ends[...].astype(BF16), rad_use[rad], (((0,), (0,)), ((), ())), preferred_element_type=F32
-    )
-    high, low = halves(fields[...])
-    pairs = jnp.concatenate([high.reshape(rows, cells_r), low.reshape(rows, cells_r)], axis=1)
-    both = dot(pairs, rad_main[rad])
-    slope = (both[:, :cells_r] + both[:, cells_r:] + radial_rim) * radial_metric[...]
-    grad_radial[...] = slope.reshape(planes, cells_t, cells_r)
-    for p in range(planes):
+    for p in range(chunk):
         group, slot = divmod(p, PACK)
+        group = step * (chunk // PACK) + group
         rims[p, 0:EDGE, :] = from_left[group, EDGE * slot : EDGE * (slot + 1), :]
         rims[p, 8 : 8 + EDGE, :] = from_right[group, EDGE * slot : EDGE * (slot + 1), :]
-    for p in range(0, planes, 2):
-        stacks = []
-        for q in (p, p + 1):
-            rim_h, rim_l = halves(rims[q])
-            stacks.append(
-                jnp.concatenate([high[q], high[q], low[q], rim_h, rim_h, rim_l], axis=0)
-            )
-        result = dot(azi_main[...], jnp.concatenate(stacks, axis=1))
+    high, low = halves(rims[...])
+    for p in range(0, chunk, 2):
+        result = dot(azi_use[...], stacked(high, low, p).astype(BF16))
         for k, q in enumerate((p, p + 1)):
             lanes = slice(k * cells_r, (k + 1) * cells_r)
-            grad_azimuth[q] = result[:cells_t, lanes] * azimuth_metric[...]
-            filtered[q] = result[cells_t:, lanes]
+            slope = part_slope[step * chunk + q] + result[:cells_t, lanes]
+            grad_azimuth[q] = slope * azimuth_metric[...]
+            filtered[q] = part_smooth[step * chunk + q] + result[cells_t:, lanes]
+
+    @pl.when(step == pl.num_programs(0) - 1)
+    def _():
+        copy.wait()
 
 
 def local(tables, azi_count, rad_count, fields, radial_metric, azimuth_metric):
-    azi_send, azi_main, rad_send, rad_main, rad_use = [jnp.asarray(t) for t in tables]
+    azi_send, azi_main, azi_use, rad_send, rad_main, rad_use = [jnp.asarray(t) for t in tables]
     shape = fields.shape
     cells_t, cells_r = shape[2], shape[3]
     planes = shape[0] * shape[1]
     x = fields.reshape(planes, cells_t, cells_r)
     chunk = 8
-    steps = planes // chunk
+    count = planes // chunk
     rims = jax.ShapeDtypeStruct((planes // PACK, PACK * EDGE, cells_r), F32)
-    ends = jax.ShapeDtypeStruct((2, planes * cells_t), F32)
-    hbm = pl.BlockSpec(memory_space=pl.ANY)
+    full = jax.ShapeDtypeStruct(x.shape, F32)
+    ends = pltpu.VMEM((2, planes * cells_t), F32)
+    hbm = pl.BlockSpec(memory_space=pltpu.HBM)
     vmem = pl.BlockSpec(memory_space=pltpu.VMEM)
-    from_left, from_right, from_in, from_out = pl.pallas_call(
-        functools.partial(exchange_kernel, azi_count, rad_count, chunk),
-        out_shape=[rims, rims, ends, ends],
-        in_specs=[hbm, vmem, vmem],
-        out_specs=[hbm] * 4,
+    dma = pltpu.SemaphoreType.DMA
+    from_left, from_right, part_slope, part_smooth, radial = pl.pallas_call(
+        functools.partial(block_kernel, azi_count, rad_count, chunk),
+        out_shape=[rims, rims, full, full, full],
+        in_specs=[hbm] * 7,
+        out_specs=[vmem] * 5,
         scratch_shapes=[
             pltpu.VMEM(x.shape, F32),
+            pltpu.VMEM(azi_send.shape, BF16),
+            pltpu.VMEM(azi_main.shape, BF16),
+            pltpu.VMEM(rad_send.shape[1:], BF16),
+            pltpu.VMEM(rad_main.shape[1:], BF16),
+            pltpu.VMEM(rad_use.shape[1:], BF16),
+            pltpu.VMEM((1, cells_r), F32),
             pltpu.VMEM(rims.shape, F32),
             pltpu.VMEM(rims.shape, F32),
-            pltpu.VMEM(ends.shape, F32),
-            pltpu.VMEM(ends.shape, F32),
-            pltpu.SemaphoreType.DMA((steps,)),
-            pltpu.SemaphoreType.DMA((4,)),
-            pltpu.SemaphoreType.DMA((4,)),
+            ends,
+            ends,
+            ends,
+            ends,
+            pltpu.VMEM((16, chunk * cells_t), F32),
+            dma((6,)),
+            dma((count,)),
+            dma((2, count)),
+            dma((2, count)),
+            dma((2,)),
+            dma((2,)),
         ],
         compiler_params=pltpu.CompilerParams(
-            collective_id=0, has_side_effects=True, vmem_limit_bytes=32 * 2**20
+            collective_id=0, has_side_effects=True, vmem_limit_bytes=24 * 2**20
         ),
-    )(x, azi_send, rad_send)
-
-    def whole(a):
-        return pl.BlockSpec(a.shape, lambda i: (0,) * a.ndim)
+    )(
+        *[
+            pltpu.with_memory_space_constraint(a, pltpu.HBM)
+            for a in (x, azi_send, azi_main, rad_send, rad_main, rad_use, radial_metric.reshape(1, cells_r))
+        ]
+    )
 
     part = pl.BlockSpec((chunk, cells_t, cells_r), lambda i: (i, 0, 0))
-    rim_part = pl.BlockSpec((chunk // PACK, PACK * EDGE, cells_r), lambda i: (i, 0, 0))
-    end_part = pl.BlockSpec((2, chunk * cells_t), lambda i: (0, i))
-    metrics = (azimuth_metric.reshape(1, cells_r), radial_metric.reshape(1, cells_r))
     outs = pl.pallas_call(
-        solve_kernel,
-        grid=(steps,),
-        out_shape=[jax.ShapeDtypeStruct(x.shape, F32)] * 3,
-        in_specs=[part, rim_part, rim_part, end_part, end_part]
-        + [whole(a) for a in (azi_main, rad_main, rad_use) + metrics],
-        out_specs=[part] * 3,
-        scratch_shapes=[
-            pltpu.VMEM((chunk, 16, cells_r), F32),
-            pltpu.VMEM((16, chunk * cells_t), F32),
-        ],
-        compiler_params=pltpu.CompilerParams(vmem_limit_bytes=32 * 2**20),
-    )(x, from_left, from_right, from_in, from_out, azi_main, rad_main, rad_use, *metrics)
-    return tuple(a.reshape(shape) for a in outs)
+        functools.partial(join_kernel, chunk),
+        grid=(count,),
+        out_shape=[full] * 3,
+        in_specs=[vmem] * 7,
+        out_specs=[part, part, hbm],
+        scratch_shapes=[pltpu.VMEM((chunk, 16, cells_r), F32), dma],
+        compiler_params=pltpu.CompilerParams(vmem_limit_bytes=24 * 2**20),
+    )(
+        part_slope, part_smooth, radial, from_left, from_right, azi_use,
+        azimuth_metric.reshape(1, cells_r),
+    )
+    grad_azimuth, filtered, grad_radial = [a.reshape(shape) for a in outs]
+    return grad_azimuth, grad_radial, filtered
 
 
 def solution(mesh):

time: 18.6 us -> 16.5 us (0.89)
  the two profiles are of different devices: /device:TPU:0 before, /device:TPU:1 now
where the time goes in v2:
time: 16.5 us; the launch traced here: 16.3 us
  Pallas kernels  15.7 us (95%)
  between operations  0.67 us (4%)
    pallas_call x1, Pallas kernels, local(): pl.pallas_call(functools.partial(block_kernel, azi_count, rad_count, chun...  12.4 us
    pallas_call x1, Pallas kernels, local(): pl.pallas_call(functools.partial(join_kernel, chunk), grid=(count,), out_...  3.28 us

profile of v2, /device:TPU:1, one launch (start us, length us, event | category | flops | bytes accessed | tf_op | source)
XLA Modules:
  0.0 16.3 jit_solution(18133216018985718780)
XLA Ops:
  0.6 0.0 copy-start
  0.6 0.0 copy-start.1
  0.7 12.4 %shard_map.112 = (f32[10,24,128]{2,1,0:T(8,128)S(1)}, f32[10,24,128]{2,1,0:T(8,128)S(1)}, f32[40,64,128]{2,1,0:T(8,128)S(1)}, f32[40,64,128]{2,1,0:T(8,128)S(1)}, f32[40,64,128]{2,1,0:T(8,128)S(1)}) custom-call(f32[40,64,128]{2,1,0:T(8,128)} %bitcast.7, bf16[16,192]{1,0:T(8,128)(2,1)} %constant.12.clone.azi_send, bf16[128,192]{1,0:T(8,128)(2,1)} %constant.13.clone.azi_main, ...), custom_call_target="tpu_custom_call" | custom-call | tf_op jit(solution)/shard_map/pallas_call | solution.py:375
  13.0 0.0 copy-done
  13.1 0.0 copy-done.1
  13.1 3.3 %shard_map.113 = (f32[40,64,128]{2,1,0:T(8,128)}, f32[40,64,128]{2,1,0:T(8,128)}, f32[40,64,128]{2,1,0:T(8,128)}) custom-call(f32[40,64,128]{2,1,0:T(8,128)S(1)} %get-tuple-element.11.part_slope, f32[40,64,128]{2,1,0:T(8,128)S(1)} %get-tuple-element.12.part_smooth, f32[40,64,128]{2,1,0:T(8,128)S(1)} %get-tuple-element.13.radial, ...), custom_call_target="tpu_custom_call" | custom-call | tf_op jit(solution)/shard_map/pallas_call | solution.py:413
Async XLA Ops:
  0.6 12.4 %copy-start = (bf16[128,48]{1,0:T(8,128)(2,1)S(1)}, bf16[128,48]{1,0:T(8,128)(2,1)}, u32[]{:S(2)}) copy-start(bf16[128,48]{1,0:T(8,128)(2,1)} %constant.14.clone.azi_use) | copy-start | bytes 36868
  0.6 12.4 %copy-start.1 = (f32[128]{0:T(128)S(1)}, f32[128]{0:T(128)}, u32[]{:S(2)}) copy-start(f32[128]{0:T(128)} %param.11) | copy-start | bytes 1540

commit v3 on v2

--- a/solution.py
+++ b/solution.py
@@ -243,18 +243,20 @@
 
     edges(0)
     pl.semaphore_wait(barrier, 4)
-    for copy in sends(0):
-        copy.start()
+    sends(0)[0].start()
 
     @pl.loop(1, count)
     def _(c):
         edges(c)
-        for copy in sends(c):
-            copy.start()
+        sends(c)[0].start()
 
     @pl.loop(0, count)
     def _(c):
         radial_edges(c)
+
+    @pl.loop(0, count)
+    def _(c):
+        sends(c)[1].start()
 
     radial_copies = [
         pltpu.make_async_remote_copy(
@@ -328,34 +330,46 @@
 def join_kernel(
     chunk, part_slope, part_smooth, radial, from_left, from_right, azi_use, azimuth_metric,
     grad_azimuth, filtered, grad_radial,
-    rims, sem,
+    slopes, smooths, rims, radial_sem, sems,
 ):
-    cells_t, cells_r = part_slope.shape[1:]
-    step = pl.program_id(0)
-    copy = pltpu.make_async_copy(radial, grad_radial, sem)
-
-    @pl.when(step == 0)
-    def _():
-        copy.start()
-
+    planes, cells_t, cells_r = part_slope.shape
+    count = planes // chunk
+    groups = chunk // PACK
+    radial_copy = pltpu.make_async_copy(radial, grad_radial, radial_sem)
+    radial_copy.start()
     rims[...] = jnp.zeros_like(rims)
-    for p in range(chunk):
-        group, slot = divmod(p, PACK)
-        group = step * (chunk // PACK) + group
-        rims[p, 0:EDGE, :] = from_left[group, EDGE * slot : EDGE * (slot + 1), :]
-        rims[p, 8 : 8 + EDGE, :] = from_right[group, EDGE * slot : EDGE * (slot + 1), :]
-    high, low = halves(rims[...])
-    for p in range(0, chunk, 2):
-        result = dot(azi_use[...], stacked(high, low, p).astype(BF16))
-        for k, q in enumerate((p, p + 1)):
-            lanes = slice(k * cells_r, (k + 1) * cells_r)
-            slope = part_slope[step * chunk + q] + result[:cells_t, lanes]
-            grad_azimuth[q] = slope * azimuth_metric[...]
-            filtered[q] = part_smooth[step * chunk + q] + result[cells_t:, lanes]
-
-    @pl.when(step == pl.num_programs(0) - 1)
-    def _():
-        copy.wait()
+
+    def stores(c):
+        span = pl.ds(c * chunk, chunk)
+        return [
+            pltpu.make_async_copy(source.at[span], target.at[span], sems.at[k, c])
+            for k, (source, target) in enumerate(((slopes, grad_azimuth), (smooths, filtered)))
+        ]
+
+    @pl.loop(0, count)
+    def _(c):
+        for p in range(chunk):
+            group, slot = divmod(p, PACK)
+            span = slice(EDGE * slot, EDGE * (slot + 1))
+            rims[p, 0:EDGE, :] = from_left[c * groups + group, span, :]
+            rims[p, 8 : 8 + EDGE, :] = from_right[c * groups + group, span, :]
+        high, low = halves(rims[...])
+        for p in range(0, chunk, 2):
+            result = dot(azi_use[...], stacked(high, low, p))
+            for k in range(2):
+                q = c * chunk + p + k
+                lanes = slice(k * cells_r, (k + 1) * cells_r)
+                slopes[q] = (part_slope[q] + result[:cells_t, lanes]) * azimuth_metric[...]
+                smooths[q] = part_smooth[q] + result[cells_t:, lanes]
+        for copy in stores(c):
+            copy.start()
+
+    @pl.loop(0, count)
+    def _(c):
+        for copy in stores(c):
+            copy.wait()
+
+    radial_copy.wait()
 
 
 def local(tables, azi_count, rad_count, fields, radial_metric, azimuth_metric):
@@ -409,14 +423,18 @@
         ]
     )
 
-    part = pl.BlockSpec((chunk, cells_t, cells_r), lambda i: (i, 0, 0))
     outs = pl.pallas_call(
         functools.partial(join_kernel, chunk),
-        grid=(count,),
         out_shape=[full] * 3,
         in_specs=[vmem] * 7,
-        out_specs=[part, part, hbm],
-        scratch_shapes=[pltpu.VMEM((chunk, 16, cells_r), F32), dma],
+        out_specs=[hbm] * 3,
+        scratch_shapes=[
+            pltpu.VMEM(x.shape, F32),
+            pltpu.VMEM(x.shape, F32),
+            pltpu.VMEM((chunk, 16, cells_r), F32),
+            dma,
+            dma((2, count)),
+        ],
         compiler_params=pltpu.CompilerParams(vmem_limit_bytes=24 * 2**20),
     )(
         part_slope, part_smooth, radial, from_left, from_right, azi_use,

time: 16.5 us -> 15.5 us (0.939)
  the two profiles are of different devices: /device:TPU:1 before, /device:TPU:0 now
where the time goes in v3:
time: 15.5 us; the launch traced here: 15.4 us
  Pallas kernels  14.7 us (95%)
  between operations  0.67 us (4%)
    pallas_call x1, Pallas kernels, local(): pl.pallas_call(functools.partial(block_kernel, azi_count, rad_count, chun...  12.7 us
    pallas_call x1, Pallas kernels, local(): pl.pallas_call(functools.partial(join_kernel, chunk), out_shape=[full] *...  2.01 us

profile of v3, /device:TPU:0, one launch (start us, length us, event | category | flops | bytes accessed | tf_op | source)
XLA Modules:
  0.0 15.4 jit_solution(1186652208719859038)
XLA Ops:
  0.6 0.0 copy-start
  0.6 0.0 copy-start.1
  0.7 12.7 %shard_map.112 = (f32[10,24,128]{2,1,0:T(8,128)S(1)}, f32[10,24,128]{2,1,0:T(8,128)S(1)}, f32[40,64,128]{2,1,0:T(8,128)S(1)}, f32[40,64,128]{2,1,0:T(8,128)S(1)}, f32[40,64,128]{2,1,0:T(8,128)S(1)}) custom-call(f32[40,64,128]{2,1,0:T(8,128)} %bitcast.7, bf16[16,192]{1,0:T(8,128)(2,1)} %constant.12.clone.azi_send, bf16[128,192]{1,0:T(8,128)(2,1)} %constant.13.clone.azi_main, ...), custom_call_target="tpu_custom_call" | custom-call | tf_op jit(solution)/shard_map/pallas_call | solution.py:389
  13.4 0.0 copy-done
  13.4 0.0 copy-done.1
  13.4 2.0 %shard_map.113 = (f32[40,64,128]{2,1,0:T(8,128)}, f32[40,64,128]{2,1,0:T(8,128)}, f32[40,64,128]{2,1,0:T(8,128)}) custom-call(f32[40,64,128]{2,1,0:T(8,128)S(1)} %get-tuple-element.11.part_slope, f32[40,64,128]{2,1,0:T(8,128)S(1)} %get-tuple-element.12.part_smooth, f32[40,64,128]{2,1,0:T(8,128)S(1)} %get-tuple-element.13.radial, ...), custom_call_target="tpu_custom_call" | custom-call | tf_op jit(solution)/shard_map/pallas_call | solution.py:426
Async XLA Ops:
  0.6 12.7 %copy-start = (bf16[128,48]{1,0:T(8,128)(2,1)S(1)}, bf16[128,48]{1,0:T(8,128)(2,1)}, u32[]{:S(2)}) copy-start(bf16[128,48]{1,0:T(8,128)(2,1)} %constant.14.clone.azi_use) | copy-start | bytes 36868
  0.6 12.7 %copy-start.1 = (f32[128]{0:T(128)S(1)}, f32[128]{0:T(128)}, u32[]{:S(2)}) copy-start(f32[128]{0:T(128)} %param.11) | copy-start | bytes 1540

commit v4 on v3

--- a/solution.py
+++ b/solution.py
@@ -202,14 +202,16 @@
     tables[0].wait()
     tables[1].wait()
 
-    def sends(c):
-        span = pl.ds(c * groups, groups)
+    cuts = [0, max(1, 2 * count // 5), count]
+
+    def sends(part):
+        span = pl.ds(cuts[part] * groups, (cuts[part + 1] - cuts[part]) * groups)
         return [
             pltpu.make_async_remote_copy(
                 src_ref=source.at[span],
                 dst_ref=target.at[span],
-                send_sem=send_sem.at[k, c],
-                recv_sem=recv_sem.at[k, c],
+                send_sem=send_sem.at[k, part],
+                recv_sem=recv_sem.at[k, part],
                 device_id=place,
                 device_id_type=MESH,
             )
@@ -241,22 +243,18 @@
         to_out[:, span] = tips[0:2]
         to_in[:, span] = tips[2:4]
 
-    edges(0)
-    pl.semaphore_wait(barrier, 4)
-    sends(0)[0].start()
-
-    @pl.loop(1, count)
-    def _(c):
-        edges(c)
-        sends(c)[0].start()
+    azimuth_copies = []
+    for part in range(2):
+        pl.loop(cuts[part], cuts[part + 1])(edges)
+        if part == 0:
+            pl.semaphore_wait(barrier, 4)
+        for copy in sends(part):
+            copy.start()
+            azimuth_copies.append(copy)
 
     @pl.loop(0, count)
     def _(c):
         radial_edges(c)
-
-    @pl.loop(0, count)
-    def _(c):
-        sends(c)[1].start()
 
     radial_copies = [
         pltpu.make_async_remote_copy(
@@ -309,10 +307,8 @@
         slope = (both[:, :cells_r] + both[:, cells_r:] + outside) * metric[...]
         grad_radial[pl.ds(c * chunk, chunk)] = slope.reshape(chunk, cells_t, cells_r)
 
-    @pl.loop(0, count)
-    def _(c):
-        for copy in sends(c):
-            copy.wait()
+    for copy in azimuth_copies:
+        copy.wait()
 
 
 def stacked(high, low, p):
@@ -408,8 +404,8 @@
             pltpu.VMEM((16, chunk * cells_t), F32),
             dma((6,)),
             dma((count,)),
-            dma((2, count)),
-            dma((2, count)),
+            dma((2, 2)),
+            dma((2, 2)),
             dma((2,)),
             dma((2,)),
         ],

time: 15.5 us -> 14.9 us (0.961)
  the two profiles are of different devices: /device:TPU:0 before, /device:TPU:1 now
where the time goes in v4:
time: 14.9 us; the launch traced here: 14.8 us
  Pallas kernels  14.1 us (95%)
  between operations  0.67 us (4%)
    pallas_call x1, Pallas kernels, local(): pl.pallas_call(functools.partial(block_kernel, azi_count, rad_count, chun...  12.1 us
    pallas_call x1, Pallas kernels, local(): pl.pallas_call(functools.partial(join_kernel, chunk), out_shape=[full] *...  2.01 us

profile of v4, /device:TPU:1, one launch (start us, length us, event | category | flops | bytes accessed | tf_op | source)
XLA Modules:
  0.0 14.8 jit_solution(18045790727303286812)
XLA Ops:
  0.6 0.0 copy-start
  0.6 0.0 copy-start.1
  0.7 12.1 %shard_map.112 = (f32[10,24,128]{2,1,0:T(8,128)S(1)}, f32[10,24,128]{2,1,0:T(8,128)S(1)}, f32[40,64,128]{2,1,0:T(8,128)S(1)}, f32[40,64,128]{2,1,0:T(8,128)S(1)}, f32[40,64,128]{2,1,0:T(8,128)S(1)}) custom-call(f32[40,64,128]{2,1,0:T(8,128)} %bitcast.7, bf16[16,192]{1,0:T(8,128)(2,1)} %constant.12.clone.azi_send, bf16[128,192]{1,0:T(8,128)(2,1)} %constant.13.clone.azi_main, ...), custom_call_target="tpu_custom_call" | custom-call | tf_op jit(solution)/shard_map/pallas_call | solution.py:385
  12.7 0.0 copy-done
  12.7 0.0 copy-done.1
  12.8 2.0 %shard_map.113 = (f32[40,64,128]{2,1,0:T(8,128)}, f32[40,64,128]{2,1,0:T(8,128)}, f32[40,64,128]{2,1,0:T(8,128)}) custom-call(f32[40,64,128]{2,1,0:T(8,128)S(1)} %get-tuple-element.11.part_slope, f32[40,64,128]{2,1,0:T(8,128)S(1)} %get-tuple-element.12.part_smooth, f32[40,64,128]{2,1,0:T(8,128)S(1)} %get-tuple-element.13.radial, ...), custom_call_target="tpu_custom_call" | custom-call | tf_op jit(solution)/shard_map/pallas_call | solution.py:422
Async XLA Ops:
  0.6 12.1 %copy-start = (bf16[128,48]{1,0:T(8,128)(2,1)S(1)}, bf16[128,48]{1,0:T(8,128)(2,1)}, u32[]{:S(2)}) copy-start(bf16[128,48]{1,0:T(8,128)(2,1)} %constant.14.clone.azi_use) | copy-start | bytes 36868
  0.6 12.1 %copy-start.1 = (f32[128]{0:T(128)S(1)}, f32[128]{0:T(128)}, u32[]{:S(2)}) copy-start(f32[128]{0:T(128)} %param.11) | copy-start | bytes 1540

commit v5 on v4

--- a/solution.py
+++ b/solution.py
@@ -248,9 +248,10 @@
         pl.loop(cuts[part], cuts[part + 1])(edges)
         if part == 0:
             pl.semaphore_wait(barrier, 4)
-        for copy in sends(part):
-            copy.start()
-            azimuth_copies.append(copy)
+        rightward, leftward = sends(part)
+        azimuth_copies += [rightward, leftward]
+        rightward.start()
+        pl.when(azi != azi_count - 1)(leftward.start)
 
     @pl.loop(0, count)
     def _(c):
@@ -285,6 +286,8 @@
                 part_slope[c * chunk + p + k] = result[:cells_t, lanes]
                 part_smooth[c * chunk + p + k] = result[cells_t:, lanes]
 
+    for leftward in azimuth_copies[1::2]:
+        pl.when(azi == azi_count - 1)(leftward.start)
     for copy in radial_copies:
         copy.wait()
 

time: 14.9 us -> 14.9 us (level)
  no operation moved by 1% of the time
where the time goes in v5:
time: 14.9 us; the launch traced here: 14.8 us
  Pallas kernels  14.1 us (95%)
  between operations  0.67 us (4%)
    pallas_call x1, Pallas kernels, local(): pl.pallas_call(functools.partial(block_kernel, azi_count, rad_count, chun...  12.1 us
    pallas_call x1, Pallas kernels, local(): pl.pallas_call(functools.partial(join_kernel, chunk), out_shape=[full] *...  2.01 us

profile of v5, /device:TPU:1, one launch (start us, length us, event | category | flops | bytes accessed | tf_op | source)
XLA Modules:
  0.0 14.8 jit_solution(2783294763323100884)
XLA Ops:
  0.6 0.0 copy-start
  0.6 0.0 copy-start.1
  0.7 12.1 %shard_map.112 = (f32[10,24,128]{2,1,0:T(8,128)S(1)}, f32[10,24,128]{2,1,0:T(8,128)S(1)}, f32[40,64,128]{2,1,0:T(8,128)S(1)}, f32[40,64,128]{2,1,0:T(8,128)S(1)}, f32[40,64,128]{2,1,0:T(8,128)S(1)}) custom-call(f32[40,64,128]{2,1,0:T(8,128)} %bitcast.7, bf16[16,192]{1,0:T(8,128)(2,1)} %constant.12.clone.azi_send, bf16[128,192]{1,0:T(8,128)(2,1)} %constant.13.clone.azi_main, ...), custom_call_target="tpu_custom_call" | custom-call | tf_op jit(solution)/shard_map/pallas_call | solution.py:388
  12.7 0.0 copy-done
  12.7 0.0 copy-done.1
  12.8 2.0 %shard_map.113 = (f32[40,64,128]{2,1,0:T(8,128)}, f32[40,64,128]{2,1,0:T(8,128)}, f32[40,64,128]{2,1,0:T(8,128)}) custom-call(f32[40,64,128]{2,1,0:T(8,128)S(1)} %get-tuple-element.11.part_slope, f32[40,64,128]{2,1,0:T(8,128)S(1)} %get-tuple-element.12.part_smooth, f32[40,64,128]{2,1,0:T(8,128)S(1)} %get-tuple-element.13.radial, ...), custom_call_target="tpu_custom_call" | custom-call | tf_op jit(solution)/shard_map/pallas_call | solution.py:425
Async XLA Ops:
  0.6 12.1 %copy-start = (bf16[128,48]{1,0:T(8,128)(2,1)S(1)}, bf16[128,48]{1,0:T(8,128)(2,1)}, u32[]{:S(2)}) copy-start(bf16[128,48]{1,0:T(8,128)(2,1)} %constant.14.clone.azi_use) | copy-start | bytes 36868
  0.6 12.1 %copy-start.1 = (f32[128]{0:T(128)S(1)}, f32[128]{0:T(128)}, u32[]{:S(2)}) copy-start(f32[128]{0:T(128)} %param.11) | copy-start | bytes 1540

commit v6 on v4

--- a/solution.py
+++ b/solution.py
@@ -202,7 +202,7 @@
     tables[0].wait()
     tables[1].wait()
 
-    cuts = [0, max(1, 2 * count // 5), count]
+    cuts = [0, count]
 
     def sends(part):
         span = pl.ds(cuts[part] * groups, (cuts[part + 1] - cuts[part]) * groups)
@@ -244,7 +244,7 @@
         to_in[:, span] = tips[2:4]
 
     azimuth_copies = []
-    for part in range(2):
+    for part in range(len(cuts) - 1):
         pl.loop(cuts[part], cuts[part + 1])(edges)
         if part == 0:
             pl.semaphore_wait(barrier, 4)
@@ -404,8 +404,8 @@
             pltpu.VMEM((16, chunk * cells_t), F32),
             dma((6,)),
             dma((count,)),
-            dma((2, 2)),
-            dma((2, 2)),
+            dma((2, 1)),
+            dma((2, 1)),
             dma((2,)),
             dma((2,)),
         ],

time: 14.9 us -> 14.4 us (0.966)
  Pallas kernels: 14.1 us -> 13.5 us
    pallas_call x1, Pallas kernels: 12.1 us -> 11.5 us  [local(): pl.pallas_call(functools.partial(block_kernel, azi_count, rad_count, chun...]
where the time goes in v6:
time: 14.4 us; the launch traced here: 14.2 us
  Pallas kernels  13.5 us (94%)
  between operations  0.67 us (5%)
    pallas_call x1, Pallas kernels, local(): pl.pallas_call(functools.partial(block_kernel, azi_count, rad_count, chun...  11.5 us
    pallas_call x1, Pallas kernels, local(): pl.pallas_call(functools.partial(join_kernel, chunk), out_shape=[full] *...  2.01 us

profile of v6, /device:TPU:1, one launch (start us, length us, event | category | flops | bytes accessed | tf_op | source)
XLA Modules:
  0.0 14.2 jit_solution(6562844223887259499)
XLA Ops:
  0.6 0.0 copy-start
  0.6 0.0 copy-start.1
  0.7 11.5 %shard_map.112 = (f32[10,24,128]{2,1,0:T(8,128)S(1)}, f32[10,24,128]{2,1,0:T(8,128)S(1)}, f32[40,64,128]{2,1,0:T(8,128)S(1)}, f32[40,64,128]{2,1,0:T(8,128)S(1)}, f32[40,64,128]{2,1,0:T(8,128)S(1)}) custom-call(f32[40,64,128]{2,1,0:T(8,128)} %bitcast.7, bf16[16,192]{1,0:T(8,128)(2,1)} %constant.12.clone.azi_send, bf16[128,192]{1,0:T(8,128)(2,1)} %constant.13.clone.azi_main, ...), custom_call_target="tpu_custom_call" | custom-call | tf_op jit(solution)/shard_map/pallas_call | solution.py:385
  12.2 0.0 copy-done
  12.2 0.0 copy-done.1
  12.2 2.0 %shard_map.113 = (f32[40,64,128]{2,1,0:T(8,128)}, f32[40,64,128]{2,1,0:T(8,128)}, f32[40,64,128]{2,1,0:T(8,128)}) custom-call(f32[40,64,128]{2,1,0:T(8,128)S(1)} %get-tuple-element.11.part_slope, f32[40,64,128]{2,1,0:T(8,128)S(1)} %get-tuple-element.12.part_smooth, f32[40,64,128]{2,1,0:T(8,128)S(1)} %get-tuple-element.13.radial, ...), custom_call_target="tpu_custom_call" | custom-call | tf_op jit(solution)/shard_map/pallas_call | solution.py:422
Async XLA Ops:
  0.6 11.6 %copy-start = (bf16[128,48]{1,0:T(8,128)(2,1)S(1)}, bf16[128,48]{1,0:T(8,128)(2,1)}, u32[]{:S(2)}) copy-start(bf16[128,48]{1,0:T(8,128)(2,1)} %constant.14.clone.azi_use) | copy-start | bytes 36868
  0.6 11.6 %copy-start.1 = (f32[128]{0:T(128)S(1)}, f32[128]{0:T(128)}, u32[]{:S(2)}) copy-start(f32[128]{0:T(128)} %param.11) | copy-start | bytes 1540
